TPU v7x, 32 devices: a whole 2x2x4 slice. The times are simulated.
32 devices in a mesh: groups: 2 (over y), expert: 4 (over z), dp: 4 (over x, core).
Axes of the slice: x: 2, y: 2, z: 4, core: 2. Of those that a mesh axis runs over, the one named last changes fastest.
Arguments:
- inputs: bfloat16 [1024, 7168], P(('groups', 'expert', 'dp')), parts along dimension 0, may hold values from -6 to 6
- out_grads: bfloat16 [1024, 8, 2048], P(('groups', 'expert', 'dp')), parts along dimension 0, may hold values from -6 to 6
- routing: int32 [1024, 8], P(('groups', 'expert', 'dp')), parts along dimension 0, may hold values from 0 to 31, all different within a row; in each aligned block of 32 rows (0 to 31, 32 to 63, ...) at most 16 rows name the same one
- in_basis: bfloat16 [7168, 64], replicated, may hold values from -0.0625 to 0.0625
- out_basis: bfloat16 [32, 2048, 64], P('expert'), may hold values from -0.125 to 0.125
- val_bank: bfloat16 [256, 4096], P(('groups', 'dp')), parts along dimension 0, may hold values from -0.03125 to 0.03125
- val_ids: int32 [512], P('groups'), parts along dimension 0, may hold values from 0 to 127
Outputs:
- scores: float32 [1024, 256], P(('groups', 'expert', 'dp')), parts along dimension 0
There are 2 independent parts, one for each index of `groups`. A program takes and returns all parts, laid end to end along the dimension named above; an argument that names none is the same for every part. Nothing has to cross between parts.
Inputs may be any that keep to these rules, and one draw needn't show every extreme that they name: `routing`: each token names 8 different experts; among the 32 tokens of one device no expert is named by more than 16 tokens, a bound that some block reaches.
All inputs are finite; a program needn't handle non-finite values.
Results may differ from a plain program's by a relative error of at most 0.0051.
Values may be sent and summed in bfloat16 or wider, within the bound.
A program may use at most 64 MiB of HBM per device.

v0:
```python
import jax
import jax.numpy as jnp
from jax import lax
from jax.sharding import PartitionSpec as P


def local(inputs, out_grads, routing, in_basis, out_basis, val_bank, val_ids):
    tokens_here = inputs.shape[0]
    top_count = routing.shape[1]
    hidden_width = out_grads.shape[2]
    basis_width = in_basis.shape[1]
    owners = lax.axis_size("expert")
    local_experts = out_basis.shape[0]
    all_experts = owners * local_experts
    capacity = max(2, 2 * tokens_here * top_count // all_experts)
    slot_count = owners * local_experts * capacity
    pair_count = tokens_here * top_count
    expert_flat = routing.reshape(pair_count)
    onehot = (expert_flat[:, None] == jnp.arange(all_experts, dtype=jnp.int32)[None, :]).astype(
        jnp.int32
    )
    earlier = jnp.cumsum(onehot, axis=0) - onehot
    rank_in = jnp.sum(earlier * onehot, axis=1)
    slot_index = (
        expert_flat // local_experts * (local_experts * capacity)
        + expert_flat % local_experts * capacity
        + rank_in
    )
    pair_place = (slot_index[:, None] == jnp.arange(slot_count, dtype=jnp.int32)[None, :]).astype(
        jnp.bfloat16
    )
    token_place = jnp.sum(pair_place.reshape(tokens_here, top_count, slot_count), axis=1)
    grad_send = jnp.dot(
        pair_place.T,
        out_grads.reshape(pair_count, hidden_width),
        preferred_element_type=jnp.float32,
    ).astype(jnp.bfloat16)
    grad_send = grad_send.reshape(owners, local_experts * capacity, hidden_width)
    token_proj = jnp.dot(inputs, in_basis, preferred_element_type=jnp.float32).astype(jnp.bfloat16)
    slot_left = jnp.dot(token_place.T, token_proj, preferred_element_type=jnp.float32)
    left_send = slot_left.astype(jnp.bfloat16).reshape(
        owners, local_experts * capacity, basis_width
    )
    left_recv, grad_recv = (
        lax.all_to_all(left_send, "expert", split_axis=0, concat_axis=0, tiled=True),
        lax.all_to_all(grad_send, "expert", split_axis=0, concat_axis=0, tiled=True),
    )
    grouped = grad_recv.reshape(owners, local_experts, capacity, hidden_width)
    right_proj = jnp.einsum(
        "sjmf,jfr->sjmr", grouped, out_basis, preferred_element_type=jnp.float32
    ).reshape(slot_count, basis_width)
    left_wide = left_recv.reshape(slot_count, basis_width).astype(jnp.float32)
    outer = (left_wide[:, :, None] * right_proj[:, None, :]).astype(jnp.bfloat16)
    outer = outer.reshape(owners, local_experts * capacity, basis_width * basis_width)
    came_back = lax.all_to_all(outer, "expert", split_axis=0, concat_axis=0, tiled=True)
    pair_sketch = came_back.reshape(slot_count, basis_width * basis_width)
    sketch = jnp.dot(token_place, pair_sketch, preferred_element_type=jnp.float32).astype(
        jnp.bfloat16
    )
    bank_scores = lax.dot_general(
        sketch,
        lax.all_gather(val_bank, "dp", axis=0, tiled=True),
        (((1,), (1,)), ((), ())),
        preferred_element_type=jnp.float32,
    )
    bank_total = bank_scores.shape[1]
    select = (jnp.arange(bank_total, dtype=jnp.int32)[:, None] == val_ids[None, :]).astype(
        jnp.float32
    )
    return jnp.dot(bank_scores, select, precision=lax.Precision.HIGHEST)


def solution(mesh):
    return jax.shard_map(
        local,
        mesh=mesh,
        in_specs=(
            P(("groups", "expert", "dp"), None),
            P(("groups", "expert", "dp"), None, None),
            P(("groups", "expert", "dp"), None),
            P(),
            P("expert", None, None),
            P(("groups", "dp"), None),
            P("groups"),
        ),
        out_specs=P(("groups", "expert", "dp"), None),
        check_vma=False,
    )
```

profile of v0, /device:TPU:0, one launch (start us, length us, event | category | flops | bytes accessed | tf_op | source)
XLA Modules:
  0.0 207.9 jit_solution(9110219133885858370)
XLA Ops:
  6.5 0.0 copy-start
  6.5 0.9 copy.46
  7.4 0.1 eq.64
  7.5 0.1 eq.60
  7.6 0.6 reduce-window.6
  8.2 0.2 slice_reduce_fusion
  8.5 0.1 fusion.18
  8.6 0.1 reduce_sum.24
  8.7 0.2 fusion.12
  8.9 1.9 fusion.9
  10.8 0.6 copy.71
  11.5 6.3 %all-to-all-start = ((bf16[4,128,64]{1,2,0:T(8,128)(2,1)}), bf16[4,128,64]{1,2,0:T(8,128)(2,1)S(1)}, u32[]{:S(2)}, u32[]{:S(2)}) async-start(bf16[4,128,64]{1,2,0:T(8,128)(2,1)} %bitcast.53), calls=%async_computation | async-start | bytes 131072 | tf_op jit(solution)/shard_map/all_to_all | solution.py:45
  17.8 3.4 %convolution_convert_fusion.1 = bf16[512,2048]{1,0:T(8,128)(2,1)} fusion(bf16[32,8,2048]{2,1,0:T(8,128)(2,1)} %param.8, s32[256]{0:T(256)S(1)} %fusion.30), kind=kOutput, calls=%fused_computation.2 | convolution fusion | flops 538050560 | bytes 3146752 | tf_op jit(solution)/shard_map/dot_general | solution.py:33
  21.2 2.3 %all-to-all-done = bf16[4,128,64]{1,2,0:T(8,128)(2,1)S(1)} async-done(((bf16[4,128,64]{1,2,0:T(8,128)(2,1)}), bf16[4,128,64]{1,2,0:T(8,128)(2,1)S(1)}, u32[]{:S(2)}, u32[]{:S(2)}) %all-to-all-start) | async-done | bytes 65568 | tf_op jit(solution)/shard_map/all_to_all | solution.py:45
  23.5 4.4 %all-to-all-start.1 = ((bf16[4,128,2048]{2,1,0:T(8,128)(2,1)}), bf16[4,128,2048]{2,1,0:T(8,128)(2,1)}, u32[]{:S(2)}, u32[]{:S(2)}) async-start(bf16[4,128,2048]{2,1,0:T(8,128)(2,1)} %bitcast.55), calls=%async_computation.1 | async-start | bytes 4194304 | tf_op jit(solution)/shard_map/all_to_all | solution.py:46
  28.0 47.1 %all-to-all-done.1 = bf16[4,128,2048]{2,1,0:T(8,128)(2,1)} async-done(((bf16[4,128,2048]{2,1,0:T(8,128)(2,1)}), bf16[4,128,2048]{2,1,0:T(8,128)(2,1)}, u32[]{:S(2)}, u32[]{:S(2)}) %all-to-all-start.1) | async-done | bytes 2097184 | tf_op jit(solution)/shard_map/all_to_all | solution.py:46
  75.1 0.0 copy-done
  75.1 2.3 %fusion.3 = f32[4,8,16,64]{3,2,0,1:T(8,128)S(1)} fusion(bf16[8,2048,64]{1,2,0:T(8,128)(2,1)S(1)} %copy-done, bf16[4,8,16,2048]{3,2,1,0:T(8,128)(2,1)} %bitcast.3), kind=kOutput, calls=%fused_computation.6 | convolution fusion | flops 134217728 | bytes 4325376 | tf_op jit(solution)/shard_map/sjmf,jfr->sjmr/dot_general | solution.py:49
  77.4 0.1 copy.57
  77.5 3.4 %multiply_convert_fusion = bf16[512,64,64]{0,2,1:T(8,128)(2,1)} fusion(f32[512,64]{0,1:T(8,128)S(1)} %copy.57, f32[512,64]{0,1:T(8,128)S(1)} %copy_bitcast_fusion), kind=kLoop, calls=%fused_computation | loop fusion | flops 4194304 | bytes 4456448 | tf_op jit(solution)/shard_map/convert_element_type | solution.py:53
  81.0 6.9 %convert_element_type.52 = bf16[4,128,4096]{1,0,2:T(4,128)(2,1)} reshape(bf16[512,64,64]{0,2,1:T(8,128)(2,1)} %multiply_convert_fusion) | data formatting | bytes 8388608 | tf_op jit(solution)/shard_map/convert_element_type | solution.py:53
  87.9 4.7 %copy.58 = bf16[4,128,4096]{1,2,0:T(8,128)(2,1)} copy(bf16[4,128,4096]{1,0,2:T(4,128)(2,1)} %convert_element_type.52) | data formatting | bytes 8388608 | tf_op jit(solution)/shard_map/convert_element_type | solution.py:53
  92.6 4.9 %all-to-all-start.2 = ((bf16[4,128,4096]{1,2,0:T(8,128)(2,1)}), bf16[4,128,4096]{1,2,0:T(8,128)(2,1)}, u32[]{:S(2)}, u32[]{:S(2)}) async-start(bf16[4,128,4096]{1,2,0:T(8,128)(2,1)} %copy.58), calls=%async_computation.2 | async-start | bytes 8388608 | tf_op jit(solution)/shard_map/all_to_all | solution.py:55
  97.4 0.0 all-gather.2.cloned.1.call-start
  97.5 0.7 all-gather.2.cloned.1.call-update
  98.2 91.9 %all-to-all-done.2 = bf16[4,128,4096]{1,2,0:T(8,128)(2,1)} async-done(((bf16[4,128,4096]{1,2,0:T(8,128)(2,1)}), bf16[4,128,4096]{1,2,0:T(8,128)(2,1)}, u32[]{:S(2)}, u32[]{:S(2)}) %all-to-all-start.2) | async-done | bytes 4194336 | tf_op jit(solution)/shard_map/all_to_all | solution.py:55
  190.1 6.5 %copy.59 = bf16[4,128,4096]{2,1,0:T(8,128)(2,1)} copy(bf16[4,128,4096]{1,2,0:T(8,128)(2,1)} %all-to-all-done.2) | data formatting | bytes 8388608 | tf_op jit(solution)/shard_map/all_to_all | solution.py:55
  196.6 0.0 copy-start.1
  196.6 0.0 all-gather.2.cloned.1.call-done
  196.6 3.6 %fusion.8 = f32[32,128]{1,0:T(8,128)S(1)} fusion(bf16[128,4096]{1,0:T(8,128)(2,1)} %all-gather.2.cloned.1.call-done, bf16[32,512]{1,0:T(8,128)(2,1)S(1)} %fusion.12, bf16[512,4096]{1,0:T(8,128)(2,1)} %bitcast.54), kind=kOutput, calls=%fused_computation.7 | convolution fusion | flops 167903232 | bytes 5292032 | tf_op jit(solution)/shard_map/dot_general | solution.py:60
  200.3 0.0 copy-done.1
  200.3 0.8 fusion.14
  (7 shorter events, 0.1 us)
Async XLA Ops:
  6.5 68.6 %copy-start = (bf16[8,2048,64]{1,2,0:T(8,128)(2,1)S(1)}, bf16[8,2048,64]{1,2,0:T(8,128)(2,1)}, u32[]{:S(2)}) copy-start(bf16[8,2048,64]{1,2,0:T(8,128)(2,1)} %param.11) | copy-start | bytes 6291460
  11.5 12.1 %all-to-all-start = ((bf16[4,128,64]{1,2,0:T(8,128)(2,1)}), bf16[4,128,64]{1,2,0:T(8,128)(2,1)S(1)}, u32[]{:S(2)}, u32[]{:S(2)}) async-start(bf16[4,128,64]{1,2,0:T(8,128)(2,1)} %bitcast.53), calls=%async_computation | async-start | bytes 131072 | tf_op jit(solution)/shard_map/all_to_all | solution.py:45
  23.5 51.6 %all-to-all-start.1 = ((bf16[4,128,2048]{2,1,0:T(8,128)(2,1)}), bf16[4,128,2048]{2,1,0:T(8,128)(2,1)}, u32[]{:S(2)}, u32[]{:S(2)}) async-start(bf16[4,128,2048]{2,1,0:T(8,128)(2,1)} %bitcast.55), calls=%async_computation.1 | async-start | bytes 4194304 | tf_op jit(solution)/shard_map/all_to_all | solution.py:46
  92.6 97.6 %all-to-all-start.2 = ((bf16[4,128,4096]{1,2,0:T(8,128)(2,1)}), bf16[4,128,4096]{1,2,0:T(8,128)(2,1)}, u32[]{:S(2)}, u32[]{:S(2)}) async-start(bf16[4,128,4096]{1,2,0:T(8,128)(2,1)} %copy.58), calls=%async_computation.2 | async-start | bytes 8388608 | tf_op jit(solution)/shard_map/all_to_all | solution.py:55
  97.4 99.2 %all-gather.2.cloned.1.call-start = ((), (), s32[]{:S(2)}) async-start(), calls=%async_computation.3 | async-start | bytes 1310720 | tf_op jit(solution)/shard_map/all_gather | solution.py:62
  196.6 3.7 %copy-start.1 = (s32[256]{0:T(256)S(1)}, s32[256]{0:T(256)}, u32[]{:S(2)}) copy-start(s32[256]{0:T(256)} %param.13) | copy-start | bytes 3076
Sparse Core Ops, SparseCore 0:
  99.8 18.1 all-gather.1
where the time goes:
time: 209 us; the launch traced here: 208 us
  waiting for transfers between devices  142 us (68%)
  local copies, waits for them, and re-layouts  20.2 us (10%)
  starting transfers between devices  15.7 us (8%)
  between operations  13.5 us (6%)
  matrix products  12.1 us (6%)
  other arithmetic  4.44 us (2%)
    all_to_all x1, waiting for transfers between devices, local(): lax.all_to_all(outer, 'expert', split_axis=0, concat_axis=0, tiled=True)  91.9 us
    all_to_all x1, waiting for transfers between devices, local(): lax.all_to_all(grad_send, 'expert', split_axis=0, concat_axis=0, tiled=True)  47.1 us
    convert_element_type x2, local copies, waits for them, and re-layouts, local(): (left_wide[:, :, None] * right_proj[:, None, :]).astype(jnp.bfloat16)  11.6 us
    all_to_all x1, local copies, waits for them, and re-layouts, local(): lax.all_to_all(outer, 'expert', split_axis=0, concat_axis=0, tiled=True)  6.48 us
    all_to_all x1, starting transfers between devices, local(): lax.all_to_all(left_send, 'expert', split_axis=0, concat_axis=0, tiled=True)  6.32 us
    all_to_all x1, starting transfers between devices, local(): lax.all_to_all(outer, 'expert', split_axis=0, concat_axis=0, tiled=True)  4.86 us
    all_to_all x1, starting transfers between devices, local(): lax.all_to_all(grad_send, 'expert', split_axis=0, concat_axis=0, tiled=True)  4.45 us
  transfers between devices with their start and end apart: 4, of which 3 were waited for; matrix products, arithmetic and copies ran while one was open for 5% of the time, Pallas kernels for 0%

commit v1 on v0

v1 whole, which is shorter than its diff:
```python
import functools

import jax
import jax.numpy as jnp
from jax import lax
from jax.experimental import pallas as pl
from jax.experimental.pallas import tpu as pltpu
from jax.sharding import PartitionSpec as P

F32, BF16, I32 = jnp.float32, jnp.bfloat16, jnp.int32
MESH = pl.DeviceIdType.MESH
NT = (((1,), (1,)), ((), ()))
TN = (((0,), (0,)), ((), ()))
CHUNKS = 2


def flip(index, mask):
    result, bit = index, 1
    while bit <= mask:
        if mask & bit:
            result = result + bit * (1 - 2 * ((index // bit) % 2))
        bit *= 2
    return result


def kernel(
    sizes, x_ref, inb_ref, og_ref, rt_ref, wt_ref, bank_ref, ids_ref, out_ref,
    xbuf, ibuf, gbuf, wbuf, rbuf, rq, acc, psend, pbuf, bbuf, bsel, lrep,
    g_send, g_recv, r_send, r_recv, p_send, p_recv, b_send, b_recv,
    wr_send, wl_send, w_recv, local_sem,
):
    groups, owners, dps, topk, experts, rank = sizes
    plane = groups * dps
    tokens = x_ref.shape[0]
    pairs = og_ref.shape[0]
    width = gbuf.shape[2]
    rows = wt_ref.shape[0] // CHUNKS
    per_chunk = experts // CHUNKS
    half_tokens = tokens // 2
    g, z, d = lax.axis_index("groups"), lax.axis_index("expert"), lax.axis_index("dp")
    me = g * dps + d
    last = owners - 1

    def place(q):
        return {"groups": q // dps, "dp": q % dps}

    barrier = pltpu.get_barrier_semaphore()
    for r in range(1, plane):
        pl.semaphore_signal(barrier, inc=1, device_id=place((me + r) % plane), device_id_type=MESH)

    @pl.when(z > 0)
    def _():
        pl.semaphore_signal(barrier, inc=1, device_id={"expert": z - 1}, device_id_type=MESH)

    @pl.when(z < last)
    def _():
        pl.semaphore_signal(barrier, inc=1, device_id={"expert": z + 1}, device_id_type=MESH)

    def slice_of(q):
        return pl.ds(pl.multiple_of(q * width, width), width)

    local = [
        pltpu.make_async_copy(x_ref, xbuf, local_sem.at[0]),
        pltpu.make_async_copy(inb_ref, ibuf, local_sem.at[1]),
        pltpu.make_async_copy(og_ref.at[:, slice_of(me)], gbuf.at[me], local_sem.at[2]),
        pltpu.make_async_copy(wt_ref.at[:, slice_of(me)], wbuf.at[z], local_sem.at[3]),
        pltpu.make_async_copy(bank_ref, bbuf.at[d], local_sem.at[4]),
    ]
    for copy in local:
        copy.start()
    rbuf[me] = jnp.zeros(rbuf.shape[1:], F32)
    rbuf[me, :, :tokens] = rt_ref[...].astype(F32)

    def w_copy(source, s, c, to, sems):
        return pltpu.make_async_remote_copy(
            src_ref=source,
            dst_ref=wbuf.at[s, pl.ds(c * rows, rows)],
            send_sem=sems.at[s * CHUNKS + c],
            recv_sem=w_recv.at[s * CHUNKS + c],
            device_id={"expert": to},
            device_id_type=MESH,
        )

    def w_passed(s, c, to, sems):
        return w_copy(wbuf.at[s, pl.ds(c * rows, rows)], s, c, to, sems)

    def g_copy(q, r):
        return pltpu.make_async_remote_copy(
            src_ref=og_ref.at[:, slice_of(q)], dst_ref=gbuf.at[me],
            send_sem=g_send.at[r], recv_sem=g_recv.at[r],
            device_id=place(q), device_id_type=MESH,
        )

    def r_copy(q, r):
        return pltpu.make_async_remote_copy(
            src_ref=rbuf.at[me], dst_ref=rbuf.at[me],
            send_sem=r_send.at[r], recv_sem=r_recv.at[r],
            device_id=place(q), device_id_type=MESH,
        )

    def p_copy(q, r):
        return pltpu.make_async_remote_copy(
            src_ref=psend.at[q], dst_ref=pbuf.at[me],
            send_sem=p_send.at[r], recv_sem=p_recv.at[r],
            device_id=place(q), device_id_type=MESH,
        )

    bits = []
    bit = dps // 2
    while bit:
        bits.append(bit)
        bit //= 2
    b_copies = []

    def b_copy(source, shard, bit):
        copy = pltpu.make_async_remote_copy(
            src_ref=source, dst_ref=bbuf.at[shard],
            send_sem=b_send.at[len(b_copies)], recv_sem=b_recv.at[shard],
            device_id={"dp": flip(d, bit)}, device_id_type=MESH,
        )
        b_copies.append(copy)
        return copy

    def b_wait(shard):
        pltpu.make_async_remote_copy(
            src_ref=bbuf.at[shard], dst_ref=bbuf.at[shard],
            send_sem=b_send.at[0], recv_sem=b_recv.at[shard],
            device_id={"dp": flip(d, 1)}, device_id_type=MESH,
        ).wait_recv()

    pl.semaphore_wait(barrier, plane - 1 + jnp.where(z > 0, 1, 0) + jnp.where(z < last, 1, 0))

    for c in range(CHUNKS):
        own = wt_ref.at[pl.ds(c * rows, rows), slice_of(me)]

        @pl.when(z > 0)
        def _(own=own, c=c):
            w_copy(own, z, c, z - 1, wl_send).start()

        @pl.when(z < last)
        def _(own=own, c=c):
            w_copy(own, z, c, z + 1, wr_send).start()

    for r in range(1, plane):
        g_copy((me + r) % plane, r).start()
        r_copy((me + r) % plane, r).start()
    for bit in bits:
        b_copy(bank_ref, d, bit).start()

    local[0].wait()
    local[1].wait()
    left = lax.dot_general(xbuf[...], ibuf[...], NT, preferred_element_type=F32)
    left = left.astype(BF16).astype(F32)
    low = lax.broadcasted_iota(I32, (tokens, 2 * rank), 1) < rank
    for i in range(rank // 2):
        lrep[:, i * 2 * rank:(i + 1) * 2 * rank] = jnp.where(
            low, left[:, 2 * i:2 * i + 1], left[:, 2 * i + 1:2 * i + 2]
        )
    acc[...] = jnp.zeros_like(acc)

    @pl.when(jnp.logical_and(z > 0, z < last))
    def _():
        def step(i, carry):
            j, c = i // CHUNKS, i % CHUNKS

            @pl.when(z - 1 - j >= 0)
            def _():
                copy = w_passed(z - 1 - j, c, z + 1, wr_send)
                copy.wait_recv()
                copy.start()

            @pl.when(z + 1 + j <= last)
            def _():
                copy = w_passed(z + 1 + j, c, z - 1, wl_send)
                copy.wait_recv()
                copy.start()

            return carry

        lax.fori_loop(0, (owners - 2) * CHUNKS, step, 0)

    for r in range(1, plane):
        r_copy((me + r) % plane, r).wait_recv()
    shift, mask = topk.bit_length() - 1, topk - 1
    spread = (
        lax.broadcasted_iota(I32, (pairs, rbuf.shape[2]), 0) >> shift
        == lax.broadcasted_iota(I32, (pairs, rbuf.shape[2]), 1)
    ).astype(F32).astype(BF16)
    mine = (
        lax.broadcasted_iota(I32, (pairs, topk), 0) & mask
        == lax.broadcasted_iota(I32, (pairs, topk), 1)
    )
    half = (lax.broadcasted_iota(I32, (pairs, 2 * rank), 1) >= rank).astype(F32)

    def routes(q, carry):
        named = lax.dot_general(spread, rbuf[q].astype(BF16), NT, preferred_element_type=F32)
        named = jnp.sum(jnp.where(mine, named, 0.0), axis=1, keepdims=True)
        rq[q] = named - half
        return carry

    lax.fori_loop(0, plane, routes, 0)

    masks = [m for b in bits for m in range(1, dps) if m & -m == b]
    for m in masks:
        b_wait(flip(d, m))
        for bit in bits:
            if bit < (m & -m):
                b_copy(bbuf.at[flip(d, m)], flip(d, m), bit).start()
    local[4].wait()
    bank_rows = dps * bank_ref.shape[0]
    select = (
        lax.broadcasted_iota(I32, (bank_rows, ids_ref.shape[1]), 0) == ids_ref[...]
    ).astype(F32).astype(BF16)
    cut = 512

    def choose(i, carry):
        columns = pl.ds(pl.multiple_of(i * cut, cut), cut)
        whole = bbuf[:, :, columns].reshape(bank_rows, cut)
        bsel[:, columns] = lax.dot_general(
            select, whole, TN, preferred_element_type=F32
        ).astype(BF16)
        return carry

    lax.fori_loop(0, bsel.shape[1] // cut, choose, 0)

    for r in range(1, plane):
        g_copy((me + r) % plane, r).wait_recv()
    local[2].wait()
    local[3].wait()

    near = jnp.minimum(z, last - z)
    far_sign = jnp.where(z < last - z, 1, -1)

    def shard_at(j):
        paired = j <= 2 * near
        distance = jnp.where(paired, (j + 1) // 2, j - near)
        sign = jnp.where(paired, 1 - 2 * (j % 2), far_sign)
        return z + sign * distance

    at_end = jnp.logical_or(z == 0, z == last)

    def ready(j, s, c):
        @pl.when(jnp.logical_and(at_end, j > 0))
        def _():
            w_passed(s, c, flip(z, 1), wr_send).wait_recv()

    def product(q, s, c):
        base = wbuf[s, pl.ds(pl.multiple_of(c * rows, rows), rows)]
        full = lax.dot_general(gbuf[q], base, NT, preferred_element_type=F32)
        route = rq[q]
        total = acc[q]
        for i in range(rows // (2 * rank)):
            expert = (s * experts + c * per_chunk + 2 * i).astype(F32)
            total += jnp.where(route == expert, full[:, i * 2 * rank:(i + 1) * 2 * rank], 0.0)
        return total

    def unit(u, carry):
        j, c = u // CHUNKS, u % CHUNKS
        s = shard_at(j)
        ready(j, s, c)

        def one(q, inner):
            acc[q] = product(q, s, c)
            return inner

        return lax.fori_loop(0, plane, one, carry)

    units = owners * CHUNKS
    lax.fori_loop(0, units - 1, unit, 0)

    s, c = shard_at(last), CHUNKS - 1
    ready(last, s, c)
    low_half = lax.broadcasted_iota(I32, (half_tokens, 2 * rank), 1) < rank

    def finish(r, carry):
        q = (me + r) % plane
        total = product(q, s, c)
        total = jnp.sum(total.reshape(tokens, topk, 2 * rank), axis=1)
        total = total + pltpu.roll(total, rank, 1)
        psend[q] = jnp.where(low_half, total[:half_tokens], total[half_tokens:])

        @pl.when(r < plane)
        def _():
            p_copy(q, r).start()

        return carry

    lax.fori_loop(1, plane + 1, finish, 0)
    right = psend[me]
    for r in range(1, plane):
        p_copy((me + r) % plane, r).wait_recv()
        right += pbuf[(me + plane - r) % plane]
    turned = pltpu.roll(right, rank, 1)
    right = jnp.concatenate(
        [jnp.where(low_half, right, turned), jnp.where(low_half, turned, right)], axis=0
    )
    sketch = (lrep[...] * jnp.tile(right, (1, rank // 2))).astype(BF16)
    out_ref[...] = lax.dot_general(sketch, bsel[...], NT, preferred_element_type=F32)

    for r in range(1, plane):
        g_copy((me + r) % plane, r).wait_send()
        r_copy((me + r) % plane, r).wait_send()
        p_copy((me + r) % plane, r).wait_send()
    for copy in b_copies:
        copy.wait_send()

    def sent(i, carry):
        s, c = i // CHUNKS, i % CHUNKS

        @pl.when(jnp.logical_and(z < last, s <= z))
        def _():
            w_passed(s, c, z + 1, wr_send).wait_send()

        @pl.when(jnp.logical_and(z > 0, s >= z))
        def _():
            w_passed(s, c, z - 1, wl_send).wait_send()

        return carry

    lax.fori_loop(0, units, sent, 0)


def local(inputs, out_grads, routing, in_basis, out_basis, val_bank, val_ids):
    tokens, model = inputs.shape
    topk, hidden = out_grads.shape[1:]
    experts, _, rank = out_basis.shape
    groups, owners, dps = (lax.axis_size(a) for a in ("groups", "expert", "dp"))
    plane = groups * dps
    pairs = tokens * topk
    width = hidden // plane
    flat = val_bank.shape[1]
    count = val_ids.shape[0]
    dma = pltpu.SemaphoreType.DMA
    hbm = pl.BlockSpec(memory_space=pl.ANY)
    vmem = pl.BlockSpec(memory_space=pltpu.VMEM)
    return pl.pallas_call(
        functools.partial(kernel, (groups, owners, dps, topk, experts, rank)),
        out_shape=jax.ShapeDtypeStruct((tokens, count), F32),
        in_specs=[hbm, hbm, hbm, vmem, hbm, hbm, vmem],
        out_specs=vmem,
        scratch_shapes=[
            pltpu.VMEM((tokens, model), BF16),
            pltpu.VMEM((rank, model), BF16),
            pltpu.VMEM((plane, pairs, width), BF16),
            pltpu.VMEM((owners, experts * rank, width), BF16),
            pltpu.VMEM((plane, topk, 128), F32),
            pltpu.VMEM((plane, pairs, 2 * rank), F32),
            pltpu.VMEM((plane, pairs, 2 * rank), F32),
            pltpu.VMEM((plane, tokens // 2, 2 * rank), F32),
            pltpu.VMEM((plane, tokens // 2, 2 * rank), F32),
            pltpu.VMEM((dps,) + val_bank.shape, BF16),
            pltpu.VMEM((count, flat), BF16),
            pltpu.VMEM((tokens, flat), F32),
            dma((plane,)), dma((plane,)), dma((plane,)), dma((plane,)),
            dma((plane,)), dma((plane,)), dma((dps,)), dma((dps,)),
            dma((owners * CHUNKS,)), dma((owners * CHUNKS,)), dma((owners * CHUNKS,)),
            dma((5,)),
        ],
        compiler_params=pltpu.CompilerParams(
            collective_id=0, has_side_effects=True, vmem_limit_bytes=48 * 1024 * 1024
        ),
    )(
        inputs,
        in_basis.T,
        out_grads.reshape(pairs, hidden),
        routing.T,
        out_basis.transpose(0, 2, 1).reshape(experts * rank, hidden),
        val_bank,
        val_ids.reshape(1, count),
    )


def solution(mesh):
    return jax.shard_map(
        local,
        mesh=mesh,
        in_specs=(
            P(("groups", "expert", "dp"), None),
            P(("groups", "expert", "dp"), None, None),
            P(("groups", "expert", "dp"), None),
            P(),
            P("expert", None, None),
            P(("groups", "dp"), None),
            P("groups"),
        ),
        out_specs=P(("groups", "expert", "dp"), None),
        check_vma=False,
    )
```

time: 209 us -> 53.2 us (0.25)
  waiting for transfers between devices: 142 us -> 0 us
  Pallas kernels: 0 us -> 44.9 us
  starting transfers between devices: 15.7 us -> 0 us
  between operations: 13.5 us -> 0.02 us
  local copies, waits for them, and re-layouts: 20.2 us -> 7.94 us
  matrix products: 12.1 us -> 0 us
  other arithmetic: 4.44 us -> 0 us
    all_to_all x3 -> x0, waiting for transfers between devices: 141 us -> none  [the longest x1 91.9 us: local(): lax.all_to_all(outer, 'expert', split_axis=0, concat_axis=0, tiled=True)]
    pallas_call x0 -> x1, Pallas kernels: none -> 44.9 us  [local(): pl.pallas_call(functools.partial(kernel, (groups, owners, dps, topk, expe...]
    all_to_all x3 -> x0, starting transfers between devices: 15.6 us -> none  [the longest x1 6.32 us: local(): lax.all_to_all(left_send, 'expert', split_axis=0, concat_axis=0, tiled=True)]
    dot_general x5 -> x0, matrix products: 12.1 us -> none  [the longest x1 3.64 us: local(): lax.dot_general(sketch, lax.all_gather(val_bank, 'dp', axis=0, tiled=True...]
    convert_element_type x2 -> x0, local copies, waits for them, and re-layouts: 11.6 us -> none  [local(): (left_wide[:, :, None] * right_proj[:, None, :]).astype(jnp.bfloat16)]
    unnamed x5 -> x15, local copies, waits for them, and re-layouts: 0.92 us -> 7.94 us
    all_to_all x1 -> x0, local copies, waits for them, and re-layouts: 6.48 us -> none  [local(): lax.all_to_all(outer, 'expert', split_axis=0, concat_axis=0, tiled=True)]
    convert_element_type x3 -> x0, other arithmetic: 3.43 us -> none  [the longest x1 3.42 us: local(): (left_wide[:, :, None] * right_proj[:, None, :]).astype(jnp.bfloat16)]
  transfers between devices with their start and end apart: 4 -> 0, of which waited for: 3 -> 0; matrix products, arithmetic and copies ran while one was open for 5% -> 0% of each run, Pallas kernels for 0% -> 0%
where the time goes in v1:
time: 53.2 us; the launch traced here: 52.8 us
  Pallas kernels  44.9 us (84%)
  local copies, waits for them, and re-layouts  7.94 us (15%)
    pallas_call x1, Pallas kernels, local(): pl.pallas_call(functools.partial(kernel, (groups, owners, dps, topk, expe...  44.9 us
    unnamed x15, local copies, waits for them, and re-layouts  7.94 us

profile of v1, /device:TPU:0, one launch (start us, length us, event | category | flops | bytes accessed | tf_op | source)
XLA Modules:
  0.0 52.8 jit_solution(6319291373092041860)
XLA Ops:
  0.0 0.0 copy-start
  0.0 1.6 %copy-done = bf16[8,2048,64]{1,2,0:T(8,128)(2,1)S(1)} copy-done((bf16[8,2048,64]{1,2,0:T(8,128)(2,1)S(1)}, bf16[8,2048,64]{1,2,0:T(8,128)(2,1)}, u32[]{:S(2)}) %copy-start) | copy-done | bytes 2097176
  1.6 0.0 copy-start.1
  1.6 1.2 %copy-done.1 = bf16[32,8,2048]{2,1,0:T(8,128)(2,1)S(1)} copy-done((bf16[32,8,2048]{2,1,0:T(8,128)(2,1)S(1)}, bf16[32,8,2048]{2,1,0:T(8,128)(2,1)}, u32[]{:S(2)}) %copy-start.1) | copy-done | bytes 1048600
  2.8 0.0 copy-start.2
  2.8 1.2 %copy-done.2 = bf16[7168,64]{0,1:T(8,128)(2,1)S(1)} copy-done((bf16[7168,64]{0,1:T(8,128)(2,1)S(1)}, bf16[7168,64]{0,1:T(8,128)(2,1)}, u32[]{:S(2)}) %copy-start.2) | copy-done | bytes 917528
  4.0 0.0 copy-start.3
  4.0 1.0 %copy-done.3 = bf16[32,7168]{1,0:T(8,128)(2,1)S(1)} copy-done((bf16[32,7168]{1,0:T(8,128)(2,1)S(1)}, bf16[32,7168]{1,0:T(8,128)(2,1)}, u32[]{:S(2)}) %copy-start.3) | copy-done | bytes 458776
  5.0 0.0 copy-start.4
  5.0 0.9 %copy-done.4 = bf16[32,4096]{1,0:T(8,128)(2,1)S(1)} copy-done((bf16[32,4096]{1,0:T(8,128)(2,1)S(1)}, bf16[32,4096]{1,0:T(8,128)(2,1)}, u32[]{:S(2)}) %copy-start.4) | copy-done | bytes 262168
  6.0 0.0 copy-start.5
  6.0 0.7 %copy-done.5 = s32[32,8]{0,1:T(8,128)S(1)} copy-done((s32[32,8]{0,1:T(8,128)S(1)}, s32[32,8]{0,1:T(8,128)}, u32[]{:S(2)}) %copy-start.5) | copy-done | bytes 1048
  6.7 0.0 copy-start.6
  6.7 0.7 %copy-done.6 = s32[256]{0:T(256)S(1)} copy-done((s32[256]{0:T(256)S(1)}, s32[256]{0:T(256)}, u32[]{:S(2)}) %copy-start.6) | copy-done | bytes 1048
  7.3 44.9 %shard_map.73 = f32[32,256]{1,0:T(8,128)S(1)} custom-call(bf16[32,7168]{1,0:T(8,128)(2,1)S(1)} %copy-done.3, bf16[64,7168]{1,0:T(8,128)(2,1)S(1)} %bitcast.9, bf16[256,2048]{1,0:T(8,128)(2,1)S(1)} %bitcast.8, s32[8,32]{1,0:T(8,128)S(1)} %bitcast.10, bf16[512,2048]{1,0:T(8,128)(2,1)S(1)} %bitcast.7, bf16[32,4096]{1,0:T(8,128)(2,1)S(1)} %copy-done.4, ...), custom_call_target="tpu_custom_call" | custom-call | tf_op jit(solution)/shard_map/pallas_call | solution.py:336
  52.2 0.6 %copy.9 = f32[32,256]{1,0:T(8,128)} copy(f32[32,256]{1,0:T(8,128)S(1)} %shard_map.73) | data formatting | bytes 65536
Async XLA Ops:
  0.0 1.6 %copy-start = (bf16[8,2048,64]{1,2,0:T(8,128)(2,1)S(1)}, bf16[8,2048,64]{1,2,0:T(8,128)(2,1)}, u32[]{:S(2)}) copy-start(bf16[8,2048,64]{1,2,0:T(8,128)(2,1)} %param.11) | copy-start | bytes 6291460
  1.6 1.2 %copy-start.1 = (bf16[32,8,2048]{2,1,0:T(8,128)(2,1)S(1)}, bf16[32,8,2048]{2,1,0:T(8,128)(2,1)}, u32[]{:S(2)}) copy-start(bf16[32,8,2048]{2,1,0:T(8,128)(2,1)} %param.8) | copy-start | bytes 3145732
  2.8 1.2 %copy-start.2 = (bf16[7168,64]{0,1:T(8,128)(2,1)S(1)}, bf16[7168,64]{0,1:T(8,128)(2,1)}, u32[]{:S(2)}) copy-start(bf16[7168,64]{0,1:T(8,128)(2,1)} %param.10) | copy-start | bytes 2752516
  4.0 1.0 %copy-start.3 = (bf16[32,7168]{1,0:T(8,128)(2,1)S(1)}, bf16[32,7168]{1,0:T(8,128)(2,1)}, u32[]{:S(2)}) copy-start(bf16[32,7168]{1,0:T(8,128)(2,1)} %x_ref.1) | copy-start | bytes 1376260
  5.0 0.9 %copy-start.4 = (bf16[32,4096]{1,0:T(8,128)(2,1)S(1)}, bf16[32,4096]{1,0:T(8,128)(2,1)}, u32[]{:S(2)}) copy-start(bf16[32,4096]{1,0:T(8,128)(2,1)} %bank_ref.1) | copy-start | bytes 786436
  6.0 0.7 %copy-start.5 = (s32[32,8]{0,1:T(8,128)S(1)}, s32[32,8]{0,1:T(8,128)}, u32[]{:S(2)}) copy-start(s32[32,8]{0,1:T(8,128)} %param.9) | copy-start | bytes 3076
  6.7 0.7 %copy-start.6 = (s32[256]{0:T(256)S(1)}, s32[256]{0:T(256)}, u32[]{:S(2)}) copy-start(s32[256]{0:T(256)} %param.13) | copy-start | bytes 3076

commit v2 on v1

--- a/solution.py
+++ b/solution.py
@@ -25,7 +25,7 @@
 
 def kernel(
     sizes, x_ref, inb_ref, og_ref, rt_ref, wt_ref, bank_ref, ids_ref, out_ref,
-    xbuf, ibuf, gbuf, wbuf, rbuf, rq, acc, psend, pbuf, bbuf, bsel, lrep,
+    xbuf, ibuf, gbuf, wbuf, rbuf, rq, acc, psend, pbuf, bbuf, bsel, lrep, rt_buf, ids_buf,
     g_send, g_recv, r_send, r_recv, p_send, p_recv, b_send, b_recv,
     wr_send, wl_send, w_recv, local_sem,
 ):
@@ -35,7 +35,6 @@
     pairs = og_ref.shape[0]
     width = gbuf.shape[2]
     rows = wt_ref.shape[0] // CHUNKS
-    per_chunk = experts // CHUNKS
     half_tokens = tokens // 2
     g, z, d = lax.axis_index("groups"), lax.axis_index("expert"), lax.axis_index("dp")
     me = g * dps + d
@@ -66,10 +65,16 @@
         pltpu.make_async_copy(wt_ref.at[:, slice_of(me)], wbuf.at[z], local_sem.at[3]),
         pltpu.make_async_copy(bank_ref, bbuf.at[d], local_sem.at[4]),
     ]
+    local = [
+        pltpu.make_async_copy(rt_ref, rt_buf, local_sem.at[5]),
+        pltpu.make_async_copy(ids_ref, ids_buf, local_sem.at[6]),
+    ] + local
     for copy in local:
         copy.start()
+    local.pop(0).wait()
+    local.pop(0).wait()
     rbuf[me] = jnp.zeros(rbuf.shape[1:], F32)
-    rbuf[me, :, :tokens] = rt_ref[...].astype(F32)
+    rbuf[me, :, :tokens] = rt_buf[...].astype(F32)
 
     def w_copy(source, s, c, to, sems):
         return pltpu.make_async_remote_copy(
@@ -209,7 +214,7 @@
     local[4].wait()
     bank_rows = dps * bank_ref.shape[0]
     select = (
-        lax.broadcasted_iota(I32, (bank_rows, ids_ref.shape[1]), 0) == ids_ref[...]
+        lax.broadcasted_iota(I32, (bank_rows, ids_ref.shape[1]), 0) == ids_buf[...]
     ).astype(F32).astype(BF16)
     cut = 512
 
@@ -239,53 +244,42 @@
 
     at_end = jnp.logical_or(z == 0, z == last)
 
-    def ready(j, s, c):
+    def ready(j, s):
         @pl.when(jnp.logical_and(at_end, j > 0))
         def _():
-            w_passed(s, c, flip(z, 1), wr_send).wait_recv()
-
-    def product(q, s, c):
-        base = wbuf[s, pl.ds(pl.multiple_of(c * rows, rows), rows)]
-        full = lax.dot_general(gbuf[q], base, NT, preferred_element_type=F32)
-        route = rq[q]
+            for c in range(CHUNKS):
+                w_passed(s, c, flip(z, 1), wr_send).wait_recv()
+
+    def product(q, s):
+        full = lax.dot_general(gbuf[q], wbuf[s], NT, preferred_element_type=F32)
+        route = rq[q] - (s * experts).astype(F32)
         total = acc[q]
-        for i in range(rows // (2 * rank)):
-            expert = (s * experts + c * per_chunk + 2 * i).astype(F32)
-            total += jnp.where(route == expert, full[:, i * 2 * rank:(i + 1) * 2 * rank], 0.0)
+        for i in range(experts // 2):
+            total += jnp.where(route == 2.0 * i, full[:, i * 2 * rank:(i + 1) * 2 * rank], 0.0)
         return total
 
-    def unit(u, carry):
-        j, c = u // CHUNKS, u % CHUNKS
+    def unit(j, carry):
         s = shard_at(j)
-        ready(j, s, c)
-
-        def one(q, inner):
-            acc[q] = product(q, s, c)
-            return inner
-
-        return lax.fori_loop(0, plane, one, carry)
-
-    units = owners * CHUNKS
-    lax.fori_loop(0, units - 1, unit, 0)
-
-    s, c = shard_at(last), CHUNKS - 1
-    ready(last, s, c)
+        ready(j, s)
+        for q in range(plane):
+            acc[q] = product(q, s)
+        return carry
+
+    lax.fori_loop(0, last, unit, 0)
+
+    s = shard_at(last)
+    ready(last, s)
     low_half = lax.broadcasted_iota(I32, (half_tokens, 2 * rank), 1) < rank
 
-    def finish(r, carry):
+    for r in range(1, plane + 1):
         q = (me + r) % plane
-        total = product(q, s, c)
+        total = product(q, s)
         total = jnp.sum(total.reshape(tokens, topk, 2 * rank), axis=1)
         total = total + pltpu.roll(total, rank, 1)
         psend[q] = jnp.where(low_half, total[:half_tokens], total[half_tokens:])
-
-        @pl.when(r < plane)
-        def _():
+        if r < plane:
             p_copy(q, r).start()
 
-        return carry
-
-    lax.fori_loop(1, plane + 1, finish, 0)
     right = psend[me]
     for r in range(1, plane):
         p_copy((me + r) % plane, r).wait_recv()
@@ -317,7 +311,7 @@
 
         return carry
 
-    lax.fori_loop(0, units, sent, 0)
+    lax.fori_loop(0, owners * CHUNKS, sent, 0)
 
 
 def local(inputs, out_grads, routing, in_basis, out_basis, val_bank, val_ids):
@@ -331,12 +325,12 @@
     flat = val_bank.shape[1]
     count = val_ids.shape[0]
     dma = pltpu.SemaphoreType.DMA
-    hbm = pl.BlockSpec(memory_space=pl.ANY)
+    hbm = pl.BlockSpec(memory_space=pltpu.HBM)
     vmem = pl.BlockSpec(memory_space=pltpu.VMEM)
     return pl.pallas_call(
         functools.partial(kernel, (groups, owners, dps, topk, experts, rank)),
         out_shape=jax.ShapeDtypeStruct((tokens, count), F32),
-        in_specs=[hbm, hbm, hbm, vmem, hbm, hbm, vmem],
+        in_specs=[hbm] * 7,
         out_specs=vmem,
         scratch_shapes=[
             pltpu.VMEM((tokens, model), BF16),
@@ -351,13 +345,15 @@
             pltpu.VMEM((dps,) + val_bank.shape, BF16),
             pltpu.VMEM((count, flat), BF16),
             pltpu.VMEM((tokens, flat), F32),
+            pltpu.VMEM((topk, tokens), I32),
+            pltpu.VMEM((1, count), I32),
             dma((plane,)), dma((plane,)), dma((plane,)), dma((plane,)),
             dma((plane,)), dma((plane,)), dma((dps,)), dma((dps,)),
             dma((owners * CHUNKS,)), dma((owners * CHUNKS,)), dma((owners * CHUNKS,)),
-            dma((5,)),
+            dma((7,)),
         ],
         compiler_params=pltpu.CompilerParams(
-            collective_id=0, has_side_effects=True, vmem_limit_bytes=48 * 1024 * 1024
+            collective_id=0, has_side_effects=True, vmem_limit_bytes=60 * 1024 * 1024
         ),
     )(
         inputs,

time: 53.2 us -> 37.6 us (0.71)
  Pallas kernels: 44.9 us -> 36 us
  local copies, waits for them, and re-layouts: 7.94 us -> 1.38 us
    pallas_call x1, Pallas kernels: 44.9 us -> 36 us  [local(): pl.pallas_call(functools.partial(kernel, (groups, owners, dps, topk, expe...]
    unnamed x15 -> x1, local copies, waits for them, and re-layouts: 7.94 us -> 1.38 us
where the time goes in v2:
time: 37.6 us; the launch traced here: 37.4 us
  Pallas kernels  36 us (96%)
  local copies, waits for them, and re-layouts  1.38 us (4%)
    pallas_call x1, Pallas kernels, local(): pl.pallas_call(functools.partial(kernel, (groups, owners, dps, topk, expe...  36 us
    unnamed x1, local copies, waits for them, and re-layouts  1.38 us

profile of v2, /device:TPU:0, one launch (start us, length us, event | category | flops | bytes accessed | tf_op | source)
XLA Modules:
  0.0 37.4 jit_solution(964391743671872798)
XLA Ops:
  0.0 36.0 %shard_map.73 = f32[32,256]{1,0:T(8,128)} custom-call(bf16[32,7168]{1,0:T(8,128)(2,1)} %x_ref.1, bf16[64,7168]{1,0:T(8,128)(2,1)} %bitcast.9, bf16[256,2048]{1,0:T(8,128)(2,1)} %bitcast.8, s32[8,32]{1,0:T(8,128)} %bitcast.10, bf16[512,2048]{1,0:T(8,128)(2,1)} %bitcast.7, bf16[32,4096]{1,0:T(8,128)(2,1)} %bank_ref.1, s32[1,256]{1,0:T(1,128)} %bitcast.11), custom_call_target="tpu_custom_call" | custom-call | tf_op jit(solution)/shard_map/pallas_call | solution.py:330
  36.0 1.4 %copy.9 = f32[32,256]{1,0:T(8,128)} copy(f32[32,256]{1,0:T(8,128)} %shard_map.73) | data formatting | bytes 65536

commit v3 on v2

--- a/solution.py
+++ b/solution.py
@@ -205,34 +205,6 @@
 
     lax.fori_loop(0, plane, routes, 0)
 
-    masks = [m for b in bits for m in range(1, dps) if m & -m == b]
-    for m in masks:
-        b_wait(flip(d, m))
-        for bit in bits:
-            if bit < (m & -m):
-                b_copy(bbuf.at[flip(d, m)], flip(d, m), bit).start()
-    local[4].wait()
-    bank_rows = dps * bank_ref.shape[0]
-    select = (
-        lax.broadcasted_iota(I32, (bank_rows, ids_ref.shape[1]), 0) == ids_buf[...]
-    ).astype(F32).astype(BF16)
-    cut = 512
-
-    def choose(i, carry):
-        columns = pl.ds(pl.multiple_of(i * cut, cut), cut)
-        whole = bbuf[:, :, columns].reshape(bank_rows, cut)
-        bsel[:, columns] = lax.dot_general(
-            select, whole, TN, preferred_element_type=F32
-        ).astype(BF16)
-        return carry
-
-    lax.fori_loop(0, bsel.shape[1] // cut, choose, 0)
-
-    for r in range(1, plane):
-        g_copy((me + r) % plane, r).wait_recv()
-    local[2].wait()
-    local[3].wait()
-
     near = jnp.minimum(z, last - z)
     far_sign = jnp.where(z < last - z, 1, -1)
 
@@ -265,7 +237,22 @@
             acc[q] = product(q, s)
         return carry
 
-    lax.fori_loop(0, last, unit, 0)
+    local[2].wait()
+    local[3].wait()
+    for r in range(plane):
+        if r:
+            g_copy((me + r) % plane, r).wait_recv()
+        q = (me + plane - r) % plane
+        acc[q] = product(q, z)
+    lax.fori_loop(1, last, unit, 0)
+
+    masks = [m for b in bits for m in range(1, dps) if m & -m == b]
+    for m in masks:
+        if m & -m > 1:
+            b_wait(flip(d, m))
+            for bit in bits:
+                if bit < (m & -m):
+                    b_copy(bbuf.at[flip(d, m)], flip(d, m), bit).start()
 
     s = shard_at(last)
     ready(last, s)
@@ -279,6 +266,27 @@
         psend[q] = jnp.where(low_half, total[:half_tokens], total[half_tokens:])
         if r < plane:
             p_copy(q, r).start()
+
+    for m in masks:
+        if m & -m == 1:
+            b_wait(flip(d, m))
+    local[4].wait()
+    bank_rows = dps * bank_ref.shape[0]
+    select = (
+        lax.broadcasted_iota(I32, (bank_rows, ids_ref.shape[1]), 0) == ids_buf[...]
+    ).astype(F32).astype(BF16)
+    cut = 512
+
+    def choose(i, carry):
+        columns = pl.ds(pl.multiple_of(i * cut, cut), cut)
+        whole = bbuf[:, :, columns].reshape(bank_rows, cut)
+        bsel[:, columns] = lax.dot_general(
+            select, whole, TN, preferred_element_type=F32
+        ).astype(BF16)
+        return carry
+
+    lax.fori_loop(0, bsel.shape[1] // cut, choose, 0)
+
 
     right = psend[me]
     for r in range(1, plane):

time: 37.6 us -> 32.3 us (0.86)
  Pallas kernels: 36 us -> 30.7 us
    pallas_call x1, Pallas kernels: 36 us -> 30.7 us  [local(): pl.pallas_call(functools.partial(kernel, (groups, owners, dps, topk, expe...]
where the time goes in v3:
time: 32.3 us; the launch traced here: 32.1 us
  Pallas kernels  30.7 us (95%)
  local copies, waits for them, and re-layouts  1.38 us (4%)
    pallas_call x1, Pallas kernels, local(): pl.pallas_call(functools.partial(kernel, (groups, owners, dps, topk, expe...  30.7 us
    unnamed x1, local copies, waits for them, and re-layouts  1.38 us

profile of v3, /device:TPU:0, one launch (start us, length us, event | category | flops | bytes accessed | tf_op | source)
XLA Modules:
  0.0 32.1 jit_solution(1708343409627673326)
XLA Ops:
  0.0 30.7 %shard_map.73 = f32[32,256]{1,0:T(8,128)} custom-call(bf16[32,7168]{1,0:T(8,128)(2,1)} %x_ref.1, bf16[64,7168]{1,0:T(8,128)(2,1)} %bitcast.9, bf16[256,2048]{1,0:T(8,128)(2,1)} %bitcast.8, s32[8,32]{1,0:T(8,128)} %bitcast.10, bf16[512,2048]{1,0:T(8,128)(2,1)} %bitcast.7, bf16[32,4096]{1,0:T(8,128)(2,1)} %bank_ref.1, s32[1,256]{1,0:T(1,128)} %bitcast.11), custom_call_target="tpu_custom_call" | custom-call | tf_op jit(solution)/shard_map/pallas_call | solution.py:338
  30.7 1.4 %copy.9 = f32[32,256]{1,0:T(8,128)} copy(f32[32,256]{1,0:T(8,128)} %shard_map.73) | data formatting | bytes 65536

commit v4 on v3

--- a/solution.py
+++ b/solution.py
@@ -34,7 +34,8 @@
     tokens = x_ref.shape[0]
     pairs = og_ref.shape[0]
     width = gbuf.shape[2]
-    rows = wt_ref.shape[0] // CHUNKS
+    quarter = wt_ref.shape[0] // 4
+    bounds = ((0, 2 * quarter), (2 * quarter, 4 * quarter))
     half_tokens = tokens // 2
     g, z, d = lax.axis_index("groups"), lax.axis_index("expert"), lax.axis_index("dp")
     me = g * dps + d
@@ -76,10 +77,13 @@
     rbuf[me] = jnp.zeros(rbuf.shape[1:], F32)
     rbuf[me, :, :tokens] = rt_buf[...].astype(F32)
 
+    def part(c):
+        return pl.ds(bounds[c][0], bounds[c][1] - bounds[c][0])
+
     def w_copy(source, s, c, to, sems):
         return pltpu.make_async_remote_copy(
             src_ref=source,
-            dst_ref=wbuf.at[s, pl.ds(c * rows, rows)],
+            dst_ref=wbuf.at[s, part(c)],
             send_sem=sems.at[s * CHUNKS + c],
             recv_sem=w_recv.at[s * CHUNKS + c],
             device_id={"expert": to},
@@ -87,7 +91,7 @@
         )
 
     def w_passed(s, c, to, sems):
-        return w_copy(wbuf.at[s, pl.ds(c * rows, rows)], s, c, to, sems)
+        return w_copy(wbuf.at[s, part(c)], s, c, to, sems)
 
     def g_copy(q, r):
         return pltpu.make_async_remote_copy(
@@ -135,8 +139,11 @@
 
     pl.semaphore_wait(barrier, plane - 1 + jnp.where(z > 0, 1, 0) + jnp.where(z < last, 1, 0))
 
+    for r in range(1, plane):
+        r_copy((me + r) % plane, r).start()
+
     for c in range(CHUNKS):
-        own = wt_ref.at[pl.ds(c * rows, rows), slice_of(me)]
+        own = wt_ref.at[part(c), slice_of(me)]
 
         @pl.when(z > 0)
         def _(own=own, c=c):
@@ -148,7 +155,6 @@
 
     for r in range(1, plane):
         g_copy((me + r) % plane, r).start()
-        r_copy((me + r) % plane, r).start()
     for bit in bits:
         b_copy(bank_ref, d, bit).start()
 
@@ -161,28 +167,27 @@
         lrep[:, i * 2 * rank:(i + 1) * 2 * rank] = jnp.where(
             low, left[:, 2 * i:2 * i + 1], left[:, 2 * i + 1:2 * i + 2]
         )
-    acc[...] = jnp.zeros_like(acc)
 
     @pl.when(jnp.logical_and(z > 0, z < last))
     def _():
-        def step(i, carry):
-            j, c = i // CHUNKS, i % CHUNKS
-
-            @pl.when(z - 1 - j >= 0)
-            def _():
-                copy = w_passed(z - 1 - j, c, z + 1, wr_send)
-                copy.wait_recv()
-                copy.start()
-
-            @pl.when(z + 1 + j <= last)
-            def _():
-                copy = w_passed(z + 1 + j, c, z - 1, wl_send)
-                copy.wait_recv()
-                copy.start()
+        def step(j, carry):
+            for c in range(CHUNKS):
+
+                @pl.when(z - 1 - j >= 0)
+                def _(c=c):
+                    copy = w_passed(z - 1 - j, c, z + 1, wr_send)
+                    copy.wait_recv()
+                    copy.start()
+
+                @pl.when(z + 1 + j <= last)
+                def _(c=c):
+                    copy = w_passed(z + 1 + j, c, z - 1, wl_send)
+                    copy.wait_recv()
+                    copy.start()
 
             return carry
 
-        lax.fori_loop(0, (owners - 2) * CHUNKS, step, 0)
+        lax.fori_loop(0, owners - 2, step, 0)
 
     for r in range(1, plane):
         r_copy((me + r) % plane, r).wait_recv()
@@ -216,35 +221,42 @@
 
     at_end = jnp.logical_or(z == 0, z == last)
 
-    def ready(j, s):
+    def ready(j, s, c):
         @pl.when(jnp.logical_and(at_end, j > 0))
         def _():
-            for c in range(CHUNKS):
-                w_passed(s, c, flip(z, 1), wr_send).wait_recv()
-
-    def product(q, s):
-        full = lax.dot_general(gbuf[q], wbuf[s], NT, preferred_element_type=F32)
-        route = rq[q] - (s * experts).astype(F32)
-        total = acc[q]
-        for i in range(experts // 2):
+            w_passed(s, c, flip(z, 1), wr_send).wait_recv()
+
+    def product(q, s, total, start, stop):
+        full = lax.dot_general(gbuf[q], wbuf[s, start:stop], NT, preferred_element_type=F32)
+        route = rq[q] - (s * experts + start // rank).astype(F32)
+        for i in range((stop - start) // (2 * rank)):
             total += jnp.where(route == 2.0 * i, full[:, i * 2 * rank:(i + 1) * 2 * rank], 0.0)
         return total
 
-    def unit(j, carry):
-        s = shard_at(j)
-        ready(j, s)
-        for q in range(plane):
-            acc[q] = product(q, s)
-        return carry
-
     local[2].wait()
     local[3].wait()
+
+    def arrived(j, carry):
+        for c in range(CHUNKS):
+            ready(j, shard_at(j), c)
+        return carry
+
+    lax.fori_loop(0, last, arrived, 0)
     for r in range(plane):
         if r:
             g_copy((me + r) % plane, r).wait_recv()
         q = (me + plane - r) % plane
-        acc[q] = product(q, z)
-    lax.fori_loop(1, last, unit, 0)
+
+        def with_shard(j, total, q=q):
+            return product(q, shard_at(j), total, 0, 4 * quarter)
+
+        total = jnp.zeros(acc.shape[1:], F32)
+        if owners <= 4:
+            for j in range(last):
+                total = with_shard(j, total)
+        else:
+            total = lax.fori_loop(0, last, with_shard, total)
+        acc[q] = total
 
     masks = [m for b in bits for m in range(1, dps) if m & -m == b]
     for m in masks:
@@ -255,12 +267,15 @@
                     b_copy(bbuf.at[flip(d, m)], flip(d, m), bit).start()
 
     s = shard_at(last)
-    ready(last, s)
+    ready(last, s, 0)
+    for q in range(plane):
+        acc[q] = product(q, s, acc[q], *bounds[0])
+    ready(last, s, 1)
     low_half = lax.broadcasted_iota(I32, (half_tokens, 2 * rank), 1) < rank
 
     for r in range(1, plane + 1):
         q = (me + r) % plane
-        total = product(q, s)
+        total = product(q, s, acc[q], *bounds[1])
         total = jnp.sum(total.reshape(tokens, topk, 2 * rank), axis=1)
         total = total + pltpu.roll(total, rank, 1)
         psend[q] = jnp.where(low_half, total[:half_tokens], total[half_tokens:])
@@ -306,20 +321,20 @@
     for copy in b_copies:
         copy.wait_send()
 
-    def sent(i, carry):
-        s, c = i // CHUNKS, i % CHUNKS
-
-        @pl.when(jnp.logical_and(z < last, s <= z))
-        def _():
-            w_passed(s, c, z + 1, wr_send).wait_send()
-
-        @pl.when(jnp.logical_and(z > 0, s >= z))
-        def _():
-            w_passed(s, c, z - 1, wl_send).wait_send()
+    def sent(s, carry):
+        for c in range(CHUNKS):
+
+            @pl.when(jnp.logical_and(z < last, s <= z))
+            def _(c=c):
+                w_passed(s, c, z + 1, wr_send).wait_send()
+
+            @pl.when(jnp.logical_and(z > 0, s >= z))
+            def _(c=c):
+                w_passed(s, c, z - 1, wl_send).wait_send()
 
         return carry
 
-    lax.fori_loop(0, owners * CHUNKS, sent, 0)
+    lax.fori_loop(0, owners, sent, 0)
 
 
 def local(inputs, out_grads, routing, in_basis, out_basis, val_bank, val_ids):

time: 32.3 us -> 32 us (level)
  no operation moved by 1% of the time
where the time goes in v4:
time: 32 us; the launch traced here: 31.8 us
  Pallas kernels  30.4 us (95%)
  local copies, waits for them, and re-layouts  1.38 us (4%)
    pallas_call x1, Pallas kernels, local(): pl.pallas_call(functools.partial(kernel, (groups, owners, dps, topk, expe...  30.4 us
    unnamed x1, local copies, waits for them, and re-layouts  1.38 us

profile of v4, /device:TPU:0, one launch (start us, length us, event | category | flops | bytes accessed | tf_op | source)
XLA Modules:
  0.0 31.8 jit_solution(12331808489492718438)
XLA Ops:
  0.0 30.4 %shard_map.73 = f32[32,256]{1,0:T(8,128)} custom-call(bf16[32,7168]{1,0:T(8,128)(2,1)} %x_ref.1, bf16[64,7168]{1,0:T(8,128)(2,1)} %bitcast.9, bf16[256,2048]{1,0:T(8,128)(2,1)} %bitcast.8, s32[8,32]{1,0:T(8,128)} %bitcast.10, bf16[512,2048]{1,0:T(8,128)(2,1)} %bitcast.7, bf16[32,4096]{1,0:T(8,128)(2,1)} %bank_ref.1, s32[1,256]{1,0:T(1,128)} %bitcast.11), custom_call_target="tpu_custom_call" | custom-call | tf_op jit(solution)/shard_map/pallas_call | solution.py:353
  30.4 1.4 %copy.9 = f32[32,256]{1,0:T(8,128)} copy(f32[32,256]{1,0:T(8,128)} %shard_map.73) | data formatting | bytes 65536
